TPU v7x, 32 devices: a whole 2x2x4 slice. The times are simulated.
32 devices in a mesh: gx: 8 (over y, x, core), gy: 4 (over z).
Axes of the slice: x: 2, y: 2, z: 4, core: 2. Of those that a mesh axis runs over, the one named last changes fastest.
Arguments:
- nest_fields: float32 [5, 80, 24, 1536], P(None, None, 'gx', 'gy'), may hold values from -6 to 6
- boundary_strip: float32 [8, 5, 80, 1536], P('gx', None, None, 'gy'), may hold values from -6 to 6
- strip_owner: int32 [4], replicated, may hold values from 0 to 7, as said below
- terrain_slope: float32 [24, 1536], P('gx', 'gy'), may hold values from -0.6 to 0.6
- column_metric: float32 [24, 1536], P('gx', 'gy'), may hold values from 0.6 to 1.6
- relax_rate: float32 [24, 1536], P('gx', 'gy'), may hold values from 0.05 to 2
- parent_state: float32 [8, 512, 320], P('gx', 'gy'), may hold values from -6 to 6
- intersection_cell: int32 [8, 4, 4, 4], P('gx', 'gy'), may hold values from 0 to 127
- intersection_row: int32 [8, 4, 4, 4], P('gx', 'gy'), may hold values from 0 to 127
- intersection_count: int32 [8, 4, 4], P('gx', 'gy'), may hold values from 1 to 4, as said below
Outputs:
- nest_out: float32 [5, 80, 24, 1536], P(None, None, 'gx', 'gy')
- parent_out: float32 [8, 512, 320], P('gx', 'gy')
Inputs may be any that keep to these rules, and one draw needn't show every extreme that they name: `strip_owner`: x index that holds the boundary rows of each y block; both 0 and 7 occur. `intersection_count`: at most 4 records go from one device to one y index; in each x group one y index receives 4 records from every device of the group.
All inputs are finite; a program needn't handle non-finite values.
Results may differ from a plain program's by a relative error of at most 0.0003.
Values sent between devices are 32-bit elements; how exact they have to be, the bound alone decides.
A program may use at most 128 MiB of HBM per device.

v0:
```python
import jax
import jax.numpy as jnp
from jax import lax
from jax.sharding import PartitionSpec as P

time_step = 0.25
sound_speed = 1.0
viscosity = 0.05
buoyancy = 0.5
wind_east = 0.6
wind_north = -0.4


def broadcast(value, axis, root):
    mine = lax.axis_index(axis) == root
    return lax.psum(jnp.where(mine, value, jnp.zeros_like(value)), axis)


def padded_2(value, sides, width):
    for axis, dim in sides:
        peers, length = (lax.axis_size(axis), value.shape[dim])
        up = [(i, (i + 1) % peers) for i in range(peers - 1)]
        down = [(j, i) for i, j in up]
        last = lax.slice_in_dim(value, length - width, length, axis=dim)
        leading = lax.slice_in_dim(value, 0, width, axis=dim)
        before = lax.ppermute(last, axis, up)
        after = lax.ppermute(leading, axis, down)
        value = jnp.concatenate([before, value, after], axis=dim)
    return value


def tendency(padded, slope, metric, relax, boundary):
    center = padded[:, :, 1:-1, 1:-1]
    east_cell = padded[:, :, 2:, 1:-1]
    west_cell = padded[:, :, :-2, 1:-1]
    north_cell = padded[:, :, 1:-1, 2:]
    south_cell = padded[:, :, 1:-1, :-2]
    vertical = jnp.pad(center, ((0, 0), (1, 1), (0, 0), (0, 0)))
    along_z = 0.5 * (vertical[:, 2:] - vertical[:, :-2]) * metric
    along_x = 0.5 * (east_cell - west_cell) - slope * along_z
    along_y = 0.5 * (north_cell - south_cell)
    spread = east_cell + west_cell + north_cell + south_cell - 4.0 * center
    common = (
        -(wind_east * along_x + wind_north * along_y)
        + viscosity * spread
        + relax * (boundary[:, :, None, :] - center)
    )
    tend_east = common[0] - sound_speed * along_x[4]
    tend_north = common[1] - sound_speed * along_y[4]
    tend_vert = common[2] - sound_speed * along_z[4] + buoyancy * center[3]
    tend_heat = common[3] - buoyancy * center[2]
    tend_press = common[4] - sound_speed * (along_x[0] + along_y[1] + along_z[2])
    return jnp.stack([tend_east, tend_north, tend_vert, tend_heat, tend_press])


def on_device(
    nest_fields,
    boundary_strip,
    strip_owner,
    terrain_slope,
    column_metric,
    relax_rate,
    parent_state,
    intersection_cell,
    intersection_row,
    intersection_count,
):
    cells_x = nest_fields.shape[2]
    cells_y = nest_fields.shape[3]
    levels = nest_fields.shape[1]
    root_index = strip_owner[lax.axis_index("gy")]
    boundary = broadcast(boundary_strip, "gx", root_index)[0]
    current = nest_fields
    for weight in (1.0 / 3.0, 0.5, 1.0):
        padded = padded_2(current, (("gx", 2), ("gy", 3)), 1)
        current = nest_fields + weight * time_step * tendency(
            padded, terrain_slope, column_metric, relax_rate, boundary
        )
    feedback_fields = jnp.stack([current[0], current[1], current[3], current[4]])
    coarse = feedback_fields.reshape(4, levels, cells_x // 3, 3, cells_y // 3, 3).mean(axis=(3, 5))
    feat_width = 4 * levels
    coarse_table = coarse.transpose(2, 3, 0, 1).reshape(-1, feat_width)
    parent_cells = parent_state.shape[1]
    capacity = intersection_cell.shape[3]
    cell_ids = intersection_cell[0, 0]
    send_counts = intersection_count[0, 0]
    active = jnp.arange(capacity)[None, :] < send_counts[:, None]
    records = coarse_table[cell_ids] * active[..., None].astype(jnp.float32)
    targets = jnp.where(active, intersection_row[0, 0], parent_cells)
    got_values, got_targets = (
        lax.all_to_all(records, "gy", split_axis=0, concat_axis=0, tiled=True),
        lax.all_to_all(targets, "gy", split_axis=0, concat_axis=0, tiled=True),
    )
    flat_values = got_values.reshape(-1, feat_width)
    flat_targets = got_targets.reshape(-1)
    onehot = (flat_targets[None, :] == jnp.arange(parent_cells)[:, None]).astype(jnp.float32)
    totals = jnp.dot(onehot, flat_values, precision=lax.Precision.HIGHEST)
    record_count = jnp.sum(onehot, axis=1)
    parent_rows = parent_state[0]
    merged = jnp.where(
        record_count[:, None] > 0, totals / jnp.maximum(record_count, 1.0)[:, None], parent_rows
    )
    return (current, merged[None])


def solution(mesh):
    placed = (
        P(None, None, "gx", "gy"),
        P("gx", None, None, "gy"),
        P(),
        P("gx", "gy"),
        P("gx", "gy"),
        P("gx", "gy"),
        P("gx", "gy", None),
        P("gx", "gy", None, None),
        P("gx", "gy", None, None),
        P("gx", "gy", None),
    )
    return jax.shard_map(
        on_device,
        mesh=mesh,
        in_specs=placed,
        out_specs=(P(None, None, "gx", "gy"), P("gx", "gy", None)),
        check_vma=False,
    )
```

profile of v0, /device:TPU:6, one launch (start us, length us, event | category | flops | bytes accessed | tf_op | source)
XLA Modules:
  0.0 192.3 jit_solution(10890411660656474874)
XLA Ops:
  7.2 2.4 %fusion.40 = (f32[5,80,1,384]{3,1,2,0:T(8,128)}, f32[5,80,1,384]{3,1,2,0:T(8,128)}) fusion(f32[5,80,3,384]{3,1,2,0:T(8,128)} %param.10), kind=kLoop, calls=%fused_computation.120 | loop fusion | bytes 2457600 | tf_op jit(solution)/shard_map/slice | solution.py:24
  9.6 2.0 %collective-permute-start.1 = (f32[5,80,1,384]{3,1,2,0:T(8,128)}, f32[5,80,1,384]{3,1,2,0:T(8,128)S(1)}, u32[]{:S(2)}, u32[]{:S(2)}) collective-permute-start(f32[5,80,1,384]{3,1,2,0:T(8,128)} %get-tuple-element.26), channel_id=1, source_target_pairs={{0,4},{4,8},{8,12},{12,16},{16,20},{20,24},{24,28},{1,5},{5,9},{9,... | collective-permute-start | bytes 1843208 | tf_op jit(solution)/shard_map/ppermute | solution.py:26
  11.7 3.6 %collective-permute-start = (f32[5,80,1,384]{3,1,2,0:T(8,128)}, f32[5,80,1,384]{3,1,2,0:T(8,128)S(1)}, u32[]{:S(2)}, u32[]{:S(2)}) collective-permute-start(f32[5,80,1,384]{3,1,2,0:T(8,128)} %get-tuple-element.27), channel_id=1, source_target_pairs={{4,0},{8,4},{12,8},{16,12},{20,16},{24,20},{28,24},{5,1},{9,5},{13... | collective-permute-start | bytes 1843208 | tf_op jit(solution)/shard_map/ppermute | solution.py:27
  17.5 6.8 %collective-permute-done.1 = f32[5,80,1,384]{3,1,2,0:T(8,128)S(1)} collective-permute-done((f32[5,80,1,384]{3,1,2,0:T(8,128)}, f32[5,80,1,384]{3,1,2,0:T(8,128)S(1)}, u32[]{:S(2)}, u32[]{:S(2)}) %collective-permute-start.1) | collective-permute-done | bytes 614432 | tf_op jit(solution)/shard_map/ppermute | solution.py:26
  31.6 5.1 %collective-permute-start.3 = (f32[5,80,5,1]{1,2,3,0:T(8,128)}, f32[5,80,5,1]{1,2,3,0:T(8,128)}, u32[]{:S(2)}, u32[]{:S(2)}) collective-permute-start(f32[5,80,5,1]{1,2,3,0:T(8,128)} %copy.69), channel_id=1, source_target_pairs={{0,1},{1,2},{2,3},{4,5},{5,6},{6,7},{8,9},{9,10},{10,11},{12,13},{... | collective-permute-start | bytes 24008 | tf_op jit(solution)/shard_map/ppermute | solution.py:26
  37.8 2.1 %copy.55 = f32[5,80,5,1]{3,1,2,0:T(8,128)} copy(f32[5,80,5,1]{1,2,3,0:T(8,128)} %collective-permute-done.3) | data formatting | bytes 16000 | tf_op jit(solution)/shard_map/ppermute | solution.py:26
  39.9 33.8 %all-reduce.5.cloned.1.call-done = f32[5,80,384]{2,1,0:T(8,128)} async-done(((f32[5,80,384]{2,1,0:T(8,128)}), f32[5,80,384]{2,1,0:T(8,128)}) %all-reduce.5.cloned.1.call-update) | async-done | bytes 614416 | tf_op jit(solution)/shard_map/psum | solution.py:16
  73.6 4.0 %multiply_add_fusion.5 = (f32[5,80,3,384]{3,1,2,0:T(8,128)S(1)}, f32[5,80,3,384]{3,1,2,0:T(8,128)S(1)}, f32[5,80,3,384]{3,1,2,0:T(8,128)S(1)}, f32[5,80,3,384]{3,1,2,0:T(8,128)S(1)}) fusion(f32[5,80,3,384]{3,1,2,0:T(8,128)S(1)} %copy-done, f32[5,80,1,384]{3,1,2,0:T(8,128)} %copy-done.13, f32[5,80,1,384]{3,1,2,0:T(8,128)S(1)} %collective-permute-done.1, ...), kind=kLoop, calls=%fused_computation.40 | loop fusion | flops 11980800 | bytes 14161024 | tf_op jit(solution)/shard_map/add | solution.py:44
  80.2 2.4 %collective-permute-start.5 = (f32[5,80,1,384]{3,1,2,0:T(8,128)S(1)}, f32[5,80,1,384]{3,1,2,0:T(8,128)S(1)}, u32[]{:S(2)}, u32[]{:S(2)}) collective-permute-start(f32[5,80,1,384]{3,1,2,0:T(8,128)S(1)} %get-tuple-element.24), channel_id=1, source_target_pairs={{0,4},{4,8},{8,12},{12,16},{16,20},{20,24},{24,28},{1,5},{5,9},{9,... | collective-permute-start | bytes 1843208 | tf_op jit(solution)/shard_map/ppermute | solution.py:26
  82.7 5.2 %collective-permute-done.4 = f32[5,80,1,384]{3,1,2,0:T(8,128)S(1)} collective-permute-done((f32[5,80,1,384]{3,1,2,0:T(8,128)S(1)}, f32[5,80,1,384]{3,1,2,0:T(8,128)S(1)}, u32[]{:S(2)}, u32[]{:S(2)}) %collective-permute-start.4) | collective-permute-done | bytes 614432 | tf_op jit(solution)/shard_map/ppermute | solution.py:27
  87.9 8.6 %collective-permute-done.5 = f32[5,80,1,384]{3,1,2,0:T(8,128)S(1)} collective-permute-done((f32[5,80,1,384]{3,1,2,0:T(8,128)S(1)}, f32[5,80,1,384]{3,1,2,0:T(8,128)S(1)}, u32[]{:S(2)}, u32[]{:S(2)}) %collective-permute-start.5) | collective-permute-done | bytes 614432 | tf_op jit(solution)/shard_map/ppermute | solution.py:26
  102.0 5.1 %collective-permute-start.7 = (f32[5,80,5,1]{1,2,3,0:T(8,128)}, f32[5,80,5,1]{1,2,3,0:T(8,128)}, u32[]{:S(2)}, u32[]{:S(2)}) collective-permute-start(f32[5,80,5,1]{1,2,3,0:T(8,128)} %copy.71), channel_id=1, source_target_pairs={{0,1},{1,2},{2,3},{4,5},{5,6},{6,7},{8,9},{9,10},{10,11},{12,13},{... | collective-permute-start | bytes 24008 | tf_op jit(solution)/shard_map/ppermute | solution.py:26
  107.8 3.8 %all-to-all-start = ((s32[4,1,4]{2,1,0:T(1,128)}), s32[4,1,4]{2,1,0:T(1,128)}, u32[]{:S(2)}, u32[]{:S(2)}) async-start(s32[4,1,4]{2,1,0:T(1,128)} %bitcast.4), calls=%async_computation | async-start | bytes 4096 | tf_op jit(solution)/shard_map/all_to_all | solution.py:92
  112.0 2.1 %copy.59 = f32[5,80,5,1]{3,1,2,0:T(8,128)} copy(f32[5,80,5,1]{1,2,3,0:T(8,128)} %collective-permute-done.7) | data formatting | bytes 16000 | tf_op jit(solution)/shard_map/ppermute | solution.py:26
  114.1 7.3 %multiply_add_fusion.3 = (f32[5,80,3,384]{3,1,2,0:T(8,128)S(1)}, f32[5,80,3,384]{3,1,2,0:T(8,128)S(1)}, f32[5,80,3,384]{3,1,2,0:T(8,128)S(1)}) fusion(f32[5,80,3,384]{3,1,2,0:T(8,128)} %copy-done.3, f32[5,80,1,384]{3,1,2,0:T(8,128)S(1)} %collective-permute-done.4, f32[5,80,1,384]{3,1,2,0:T(8,128)} %copy-done.11, ...), kind=kLoop, calls=%fused_computation.37 | loop fusion | flops 13363200 | bytes 9245824 | tf_op jit(solution)/shard_map/add | solution.py:44
  127.5 2.4 %collective-permute-start.9 = (f32[5,80,1,384]{3,1,2,0:T(8,128)}, f32[5,80,1,384]{3,1,2,0:T(8,128)S(1)}, u32[]{:S(2)}, u32[]{:S(2)}) collective-permute-start(f32[5,80,1,384]{3,1,2,0:T(8,128)} %get-tuple-element.22), channel_id=1, source_target_pairs={{0,4},{4,8},{8,12},{12,16},{16,20},{20,24},{24,28},{1,5},{5,9},{9,... | collective-permute-start | bytes 1843208 | tf_op jit(solution)/shard_map/ppermute | solution.py:26
  132.2 3.3 %collective-permute-done.8 = f32[5,80,1,384]{3,1,2,0:T(8,128)S(1)} collective-permute-done((f32[5,80,1,384]{3,1,2,0:T(8,128)}, f32[5,80,1,384]{3,1,2,0:T(8,128)S(1)}, u32[]{:S(2)}, u32[]{:S(2)}) %collective-permute-start.8) | collective-permute-done | bytes 614432 | tf_op jit(solution)/shard_map/ppermute | solution.py:27
  135.4 8.3 %collective-permute-done.9 = f32[5,80,1,384]{3,1,2,0:T(8,128)S(1)} collective-permute-done((f32[5,80,1,384]{3,1,2,0:T(8,128)}, f32[5,80,1,384]{3,1,2,0:T(8,128)S(1)}, u32[]{:S(2)}, u32[]{:S(2)}) %collective-permute-start.9) | collective-permute-done | bytes 614432 | tf_op jit(solution)/shard_map/ppermute | solution.py:26
  143.8 3.2 %pad_maximum_fusion.20 = (f32[5,80,5,1]{3,1,2,0:T(8,128)}, f32[5,80,5,1]{3,1,2,0:T(8,128)}) fusion(f32[5,80,1,384]{3,1,2,0:T(8,128)S(1)} %collective-permute-done.8, f32[5,80,3,384]{3,1,2,0:T(8,128)} %copy-done.1, f32[5,80,1,384]{3,1,2,0:T(8,128)S(1)} %collective-permute-done.9), kind=kLoop, calls=%fused_computation.46 | loop fusion | flops 8000 | bytes 3088000 | tf_op jit(solution)/shard_map/concatenate | solution.py:28
  151.7 5.2 %collective-permute-start.11 = (f32[5,80,5,1]{1,2,3,0:T(8,128)S(1)}, f32[5,80,5,1]{1,2,3,0:T(8,128)}, u32[]{:S(2)}, u32[]{:S(2)}) collective-permute-start(f32[5,80,5,1]{1,2,3,0:T(8,128)S(1)} %copy.73), channel_id=1, source_target_pairs={{0,1},{1,2},{2,3},{4,5},{5,6},{6,7},{8,9},{9,10},{10,11},{12,13},{... | collective-permute-start | bytes 24008 | tf_op jit(solution)/shard_map/ppermute | solution.py:26
  157.9 2.1 %copy.63 = f32[5,80,5,1]{3,1,2,0:T(8,128)} copy(f32[5,80,5,1]{1,2,3,0:T(8,128)} %collective-permute-done.11) | data formatting | bytes 16000 | tf_op jit(solution)/shard_map/ppermute | solution.py:26
  160.0 7.3 %multiply_add_fusion.1 = (f32[5,80,3,384]{3,1,2,0:T(8,128)S(1)}, f32[5,80,3,384]{3,1,2,0:T(8,128)S(1)}, f32[5,80,3,384]{3,1,2,0:T(8,128)S(1)}) fusion(f32[5,80,3,384]{3,1,2,0:T(8,128)} %copy-done.1, f32[5,80,1,384]{3,1,2,0:T(8,128)S(1)} %collective-permute-done.8, f32[5,80,1,384]{3,1,2,0:T(8,128)} %copy-done.9, ...), kind=kLoop, calls=%fused_computation.34 | loop fusion | flops 13363200 | bytes 9245824 | tf_op jit(solution)/shard_map/add | solution.py:44
  172.9 5.8 %all-to-all-start.1 = ((f32[4,4,320]{2,1,0:T(4,128)}), f32[4,4,320]{2,1,0:T(4,128)S(1)}, u32[]{:S(2)}, u32[]{:S(2)}) async-start(f32[4,4,320]{2,1,0:T(4,128)} %broadcast_multiply_fusion.3), calls=%async_computation.1 | async-start | bytes 49152 | tf_op jit(solution)/shard_map/all_to_all | solution.py:91
  178.7 5.6 %all-to-all-done.1 = f32[4,4,320]{2,1,0:T(4,128)S(1)} async-done(((f32[4,4,320]{2,1,0:T(4,128)}), f32[4,4,320]{2,1,0:T(4,128)S(1)}, u32[]{:S(2)}, u32[]{:S(2)}) %all-to-all-start.1) | async-done | bytes 20512 | tf_op jit(solution)/shard_map/all_to_all | solution.py:91
  (131 shorter events, 39.4 us)
Async XLA Ops:
  7.2 66.4 %all-reduce.5.cloned.1.call-start = ((), (), s32[]{:S(2)}) async-start(), calls=%async_computation.2 | async-start | bytes 1228800 | tf_op jit(solution)/shard_map/psum | solution.py:16
  9.6 14.7 %copy-start = (f32[5,80,3,384]{3,1,2,0:T(8,128)S(1)}, f32[5,80,3,384]{3,1,2,0:T(8,128)}, u32[]{:S(2)}) copy-start(f32[5,80,3,384]{3,1,2,0:T(8,128)} %param.10) | copy-start | bytes 5529604
  9.6 14.7 %collective-permute-start.1 = (f32[5,80,1,384]{3,1,2,0:T(8,128)}, f32[5,80,1,384]{3,1,2,0:T(8,128)S(1)}, u32[]{:S(2)}, u32[]{:S(2)}) collective-permute-start(f32[5,80,1,384]{3,1,2,0:T(8,128)} %get-tuple-element.26), channel_id=1, source_target_pairs={{0,4},{4,8},{8,12},{12,16},{16,20},{20,24},{24,28},{1,5},{5,9},{9,... | collective-permute-start | bytes 1843208 | tf_op jit(solution)/shard_map/ppermute | solution.py:26
  11.7 12.8 %collective-permute-start = (f32[5,80,1,384]{3,1,2,0:T(8,128)}, f32[5,80,1,384]{3,1,2,0:T(8,128)S(1)}, u32[]{:S(2)}, u32[]{:S(2)}) collective-permute-start(f32[5,80,1,384]{3,1,2,0:T(8,128)} %get-tuple-element.27), channel_id=1, source_target_pairs={{4,0},{8,4},{12,8},{16,12},{20,16},{24,20},{28,24},{5,1},{9,5},{13... | collective-permute-start | bytes 1843208 | tf_op jit(solution)/shard_map/ppermute | solution.py:27
  27.3 46.3 %copy-start.14 = (f32[3,384]{1,0:T(4,128)S(1)}, f32[3,384]{1,0:T(4,128)}, u32[]{:S(2)}) copy-start(f32[3,384]{1,0:T(4,128)} %param.15) | copy-start | bytes 13828
  27.3 46.3 %copy-start.15 = (f32[3,384]{1,0:T(4,128)S(1)}, f32[3,384]{1,0:T(4,128)}, u32[]{:S(2)}) copy-start(f32[3,384]{1,0:T(4,128)} %param.13) | copy-start | bytes 13828
  29.1 7.6 %collective-permute-start.2 = (f32[5,80,5,1]{1,2,3,0:T(8,128)S(1)}, f32[5,80,5,1]{1,2,3,0:T(8,128)S(1)}, u32[]{:S(2)}, u32[]{:S(2)}) collective-permute-start(f32[5,80,5,1]{1,2,3,0:T(8,128)S(1)} %copy.68), channel_id=1, source_target_pairs={{1,0},{2,1},{3,2},{5,4},{6,5},{7,6},{9,8},{10,9},{11,10},{13,12},{... | collective-permute-start | bytes 24008 | tf_op jit(solution)/shard_map/ppermute | solution.py:27
  31.6 6.2 %collective-permute-start.3 = (f32[5,80,5,1]{1,2,3,0:T(8,128)}, f32[5,80,5,1]{1,2,3,0:T(8,128)}, u32[]{:S(2)}, u32[]{:S(2)}) collective-permute-start(f32[5,80,5,1]{1,2,3,0:T(8,128)} %copy.69), channel_id=1, source_target_pairs={{0,1},{1,2},{2,3},{4,5},{5,6},{6,7},{8,9},{9,10},{10,11},{12,13},{... | collective-permute-start | bytes 24008 | tf_op jit(solution)/shard_map/ppermute | solution.py:26
  78.2 19.6 %copy-start.3 = (f32[5,80,3,384]{3,1,2,0:T(8,128)}, f32[5,80,3,384]{3,1,2,0:T(8,128)S(1)}, u32[]{:S(2)}) copy-start(f32[5,80,3,384]{3,1,2,0:T(8,128)S(1)} %multiply_add_fusion.4) | copy-start | bytes 5529604
  78.3 9.6 %collective-permute-start.4 = (f32[5,80,1,384]{3,1,2,0:T(8,128)S(1)}, f32[5,80,1,384]{3,1,2,0:T(8,128)S(1)}, u32[]{:S(2)}, u32[]{:S(2)}) collective-permute-start(f32[5,80,1,384]{3,1,2,0:T(8,128)S(1)} %get-tuple-element.25), channel_id=1, source_target_pairs={{4,0},{8,4},{12,8},{16,12},{20,16},{24,20},{28,24},{5,1},{9,5},{13... | collective-permute-start | bytes 1843208 | tf_op jit(solution)/shard_map/ppermute | solution.py:27
  80.2 16.3 %collective-permute-start.5 = (f32[5,80,1,384]{3,1,2,0:T(8,128)S(1)}, f32[5,80,1,384]{3,1,2,0:T(8,128)S(1)}, u32[]{:S(2)}, u32[]{:S(2)}) collective-permute-start(f32[5,80,1,384]{3,1,2,0:T(8,128)S(1)} %get-tuple-element.24), channel_id=1, source_target_pairs={{0,4},{4,8},{8,12},{12,16},{16,20},{20,24},{24,28},{1,5},{5,9},{9,... | collective-permute-start | bytes 1843208 | tf_op jit(solution)/shard_map/ppermute | solution.py:26
  99.6 12.0 %collective-permute-start.6 = (f32[5,80,5,1]{1,2,3,0:T(8,128)S(1)}, f32[5,80,5,1]{1,2,3,0:T(8,128)S(1)}, u32[]{:S(2)}, u32[]{:S(2)}) collective-permute-start(f32[5,80,5,1]{1,2,3,0:T(8,128)S(1)} %copy.70), channel_id=1, source_target_pairs={{1,0},{2,1},{3,2},{5,4},{6,5},{7,6},{9,8},{10,9},{11,10},{13,12},{... | collective-permute-start | bytes 24008 | tf_op jit(solution)/shard_map/ppermute | solution.py:27
  102.0 10.0 %collective-permute-start.7 = (f32[5,80,5,1]{1,2,3,0:T(8,128)}, f32[5,80,5,1]{1,2,3,0:T(8,128)}, u32[]{:S(2)}, u32[]{:S(2)}) collective-permute-start(f32[5,80,5,1]{1,2,3,0:T(8,128)} %copy.71), channel_id=1, source_target_pairs={{0,1},{1,2},{2,3},{4,5},{5,6},{6,7},{8,9},{9,10},{10,11},{12,13},{... | collective-permute-start | bytes 24008 | tf_op jit(solution)/shard_map/ppermute | solution.py:26
  107.8 22.3 %all-to-all-start = ((s32[4,1,4]{2,1,0:T(1,128)}), s32[4,1,4]{2,1,0:T(1,128)}, u32[]{:S(2)}, u32[]{:S(2)}) async-start(s32[4,1,4]{2,1,0:T(1,128)} %bitcast.4), calls=%async_computation | async-start | bytes 4096 | tf_op jit(solution)/shard_map/all_to_all | solution.py:92
  125.6 9.9 %collective-permute-start.8 = (f32[5,80,1,384]{3,1,2,0:T(8,128)}, f32[5,80,1,384]{3,1,2,0:T(8,128)S(1)}, u32[]{:S(2)}, u32[]{:S(2)}) collective-permute-start(f32[5,80,1,384]{3,1,2,0:T(8,128)} %get-tuple-element.23), channel_id=1, source_target_pairs={{4,0},{8,4},{12,8},{16,12},{20,16},{24,20},{28,24},{5,1},{9,5},{13... | collective-permute-start | bytes 1843208 | tf_op jit(solution)/shard_map/ppermute | solution.py:27
  127.5 16.3 %collective-permute-start.9 = (f32[5,80,1,384]{3,1,2,0:T(8,128)}, f32[5,80,1,384]{3,1,2,0:T(8,128)S(1)}, u32[]{:S(2)}, u32[]{:S(2)}) collective-permute-start(f32[5,80,1,384]{3,1,2,0:T(8,128)} %get-tuple-element.22), channel_id=1, source_target_pairs={{0,4},{4,8},{8,12},{12,16},{16,20},{20,24},{24,28},{1,5},{5,9},{9,... | collective-permute-start | bytes 1843208 | tf_op jit(solution)/shard_map/ppermute | solution.py:26
  132.1 14.9 %copy-start.20 = (s32[16]{0:T(128)}, s32[16]{0:T(128)S(1)}, u32[]{:S(2)}) copy-start(s32[16]{0:T(128)S(1)} %eq.19) | copy-start | bytes 196
  132.1 24.7 %copy-start.24 = (f32[128]{0:T(128)}, f32[128]{0:T(128)S(1)}, u32[]{:S(2)}) copy-start(f32[128]{0:T(128)S(1)} %convert_reduce_fusion) | copy-start | bytes 1540
  148.7 8.8 %collective-permute-start.10 = (f32[5,80,5,1]{1,2,3,0:T(8,128)S(1)}, f32[5,80,5,1]{1,2,3,0:T(8,128)S(1)}, u32[]{:S(2)}, u32[]{:S(2)}) collective-permute-start(f32[5,80,5,1]{1,2,3,0:T(8,128)S(1)} %copy.72), channel_id=1, source_target_pairs={{1,0},{2,1},{3,2},{5,4},{6,5},{7,6},{9,8},{10,9},{11,10},{13,12},{... | collective-permute-start | bytes 24008 | tf_op jit(solution)/shard_map/ppermute | solution.py:27
  151.7 6.2 %collective-permute-start.11 = (f32[5,80,5,1]{1,2,3,0:T(8,128)S(1)}, f32[5,80,5,1]{1,2,3,0:T(8,128)}, u32[]{:S(2)}, u32[]{:S(2)}) collective-permute-start(f32[5,80,5,1]{1,2,3,0:T(8,128)S(1)} %copy.73), channel_id=1, source_target_pairs={{0,1},{1,2},{2,3},{4,5},{5,6},{6,7},{8,9},{9,10},{10,11},{12,13},{... | collective-permute-start | bytes 24008 | tf_op jit(solution)/shard_map/ppermute | solution.py:26
  170.5 13.8 %copy-start.21 = (s32[16]{0:T(128)S(1)}, s32[16]{0:T(128)}, u32[]{:S(2)}) copy-start(s32[16]{0:T(128)} %copy-done.20) | copy-start | bytes 196
  170.6 13.8 %copy-start.22 = (f32[1,128,320]{1,2,0:T(8,128)S(1)}, f32[1,128,320]{1,2,0:T(8,128)}, u32[]{:S(2)}) copy-start(f32[1,128,320]{1,2,0:T(8,128)} %param.16) | copy-start | bytes 491524
  170.6 13.8 %copy-start.26 = (pred[128]{0:T(512)(128)(4,1)S(1)}, pred[128]{0:T(512)(128)(4,1)}, u32[]{:S(2)}) copy-start(pred[128]{0:T(512)(128)(4,1)} %broadcast_compare_fusion) | copy-start | bytes 388
  172.9 11.5 %all-to-all-start.1 = ((f32[4,4,320]{2,1,0:T(4,128)}), f32[4,4,320]{2,1,0:T(4,128)S(1)}, u32[]{:S(2)}, u32[]{:S(2)}) async-start(f32[4,4,320]{2,1,0:T(4,128)} %broadcast_multiply_fusion.3), calls=%async_computation.1 | async-start | bytes 49152 | tf_op jit(solution)/shard_map/all_to_all | solution.py:91
  (18 other events, 104.0 us)
Sparse Core Ops, SparseCore 0:
  17.6 55.9 all-reduce.4
where the time goes:
time: 193 us; the launch traced here: 192 us
  waiting for transfers between devices  72.3 us (37%)
  starting transfers between devices  43.4 us (22%)
  other arithmetic  32 us (17%)
  local copies, waits for them, and re-layouts  28.3 us (15%)
  between operations  15.2 us (8%)
    psum x1, waiting for transfers between devices, broadcast(): return lax.psum(jnp.where(mine, value, jnp.zeros_like(value)), axis)  33.8 us
    ppermute x6, waiting for transfers between devices, padded_2(): before = lax.ppermute(last, axis, up)  24.4 us
    ppermute x6, starting transfers between devices, padded_2(): before = lax.ppermute(last, axis, up)  22.4 us
    add x3, other arithmetic, tendency(): -(wind_east * along_x + wind_north * along_y) + viscosity * spread  18.6 us
    unnamed x62, local copies, waits for them, and re-layouts  13.2 us
    ppermute x6, starting transfers between devices, padded_2(): after = lax.ppermute(leading, axis, down)  11.4 us
    ppermute x6, waiting for transfers between devices, padded_2(): after = lax.ppermute(leading, axis, down)  8.5 us
    ppermute x3, local copies, waits for them, and re-layouts, padded_2(): before = lax.ppermute(last, axis, up)  6.23 us
  transfers between devices with their start and end apart: 15, of which 8 were waited for; matrix products, arithmetic and copies ran while one was open for 15% of the time, Pallas kernels for 0%

commit v1 on v0

v1 whole, which is shorter than its diff:
```python
import functools
import jax
import jax.numpy as jnp
from jax import lax
from jax.experimental import pallas as pl
from jax.experimental.pallas import tpu as pltpu
from jax.sharding import PartitionSpec as P

MESH = pl.DeviceIdType.MESH
time_step = 0.25
viscosity = 0.05
buoyancy = 0.5
wind_east = 0.6
wind_north = -0.4
PAD = 8
CH = 16
HIGH = lax.Precision.HIGHEST


def kernel(
    n_gx, n_gy, cap,
    owner_ref, cell_ref, row_ref, count_ref,
    nest_ref, strip_ref, slope_ref, metric_ref, relax_ref, parent_ref,
    out_ref, pout_ref,
    q, halo, edge_out, edge_in, coef,
    strip, got_half, half, got_quarter, quarter, got_other, whole_half, got_rest, bound,
    total, records, got_records,
    load_sem, strip_sem, x_send, x_recv, y_send, y_recv, b_send, b_recv, r_send, r_recv, out_sem,
):
    fields, levels, width = q.shape[1], q.shape[3] - 2 * PAD, q.shape[4]
    chunks = levels // CH
    gx, gy = lax.axis_index("gx"), lax.axis_index("gy")
    tile = width // 3
    inner = pl.ds(PAD, levels)

    load = pltpu.make_async_copy(nest_ref, q.at[0, :, :, inner, :], load_sem)
    load.start()
    load_strip = pltpu.make_async_copy(strip_ref, strip, strip_sem)
    load_strip.start()

    barrier = pltpu.get_barrier_semaphore()
    for off in range(1, n_gx):
        pl.semaphore_signal(barrier, inc=1, device_id={"gx": lax.rem(gx + off, n_gx)}, device_id_type=MESH)
    for off in range(1, n_gy):
        pl.semaphore_signal(barrier, inc=1, device_id={"gy": lax.rem(gy + off, n_gy)}, device_id_type=MESH)

    zero = jnp.zeros((PAD, width), jnp.float32)

    def clear(s, _):
        for f in range(fields):
            for x in range(3):
                q[s, f, x, 0:PAD, :] = zero
                q[s, f, x, PAD + levels :, :] = zero
        return 0

    lax.fori_loop(0, 3, clear, 0)

    def clear_side(side):
        def body(i, _):
            for f in range(fields):
                halo[side, i // (levels // 8), f, pl.ds(pl.multiple_of(i % (levels // 8) * 8, 8), 8), :] = zero
            return 0

        lax.fori_loop(0, 3 * levels // 8, body, 0)

    @pl.when(gx == 0)
    def _():
        clear_side(0)

    @pl.when(gx == n_gx - 1)
    def _():
        clear_side(1)

    @pl.when(gy == 0)
    def _():
        edge_in[0] = jnp.zeros(edge_in.shape[1:], jnp.float32)

    @pl.when(gy == n_gy - 1)
    def _():
        edge_in[1] = jnp.zeros(edge_in.shape[1:], jnp.float32)

    for x in range(3):
        for i, ref in enumerate((slope_ref, metric_ref, relax_ref)):
            coef[i, x] = jnp.broadcast_to(ref[x : x + 1, :], (8, width))

    has_low = (gx > 0, gy > 0)
    has_high = (gx < n_gx - 1, gy < n_gy - 1)

    def x_copy(side, s, k):
        rows = pl.ds(pl.multiple_of(k * CH, 8), CH)
        padded = pl.ds(pl.multiple_of(k * CH + PAD, 8), CH)
        peer = gx + 1 if side == 0 else gx - 1
        return pltpu.make_async_remote_copy(
            src_ref=q.at[s, :, 2 if side == 0 else 0, padded, :],
            dst_ref=halo.at[side, s, :, rows, :],
            send_sem=x_send.at[side, s, k],
            recv_sem=x_recv.at[side, s, k],
            device_id={"gx": peer},
            device_id_type=MESH,
        )

    def y_copy(side, s, k):
        rows = pl.ds(pl.multiple_of(k * CH, 8), CH)
        peer = gy + 1 if side == 0 else gy - 1
        return pltpu.make_async_remote_copy(
            src_ref=edge_out.at[side, s, rows, :],
            dst_ref=edge_in.at[side, s, rows, :],
            send_sem=y_send.at[side, s, k],
            recv_sem=y_recv.at[side, s, k],
            device_id={"gy": peer},
            device_id_type=MESH,
        )

    def send(copy, s, k, axis):
        @pl.when(has_high[axis])
        def _():
            copy(0, s, k).start()

        @pl.when(has_low[axis])
        def _():
            copy(1, s, k).start()

    def received(copy, s, k, axis):
        @pl.when(has_low[axis])
        def _():
            copy(0, s, k).wait_recv()

        @pl.when(has_high[axis])
        def _():
            copy(1, s, k).wait_recv()

    def sent(copy, s, k, axis):
        @pl.when(has_high[axis])
        def _():
            copy(0, s, k).wait_send()

        @pl.when(has_low[axis])
        def _():
            copy(1, s, k).wait_send()

    lane = lax.broadcasted_iota(jnp.int32, (CH, tile), 1)

    def pack(s, k):
        rows = pl.ds(pl.multiple_of(k * CH + PAD, 8), CH)
        high = jnp.zeros((CH, tile), jnp.float32)
        low = jnp.zeros((CH, tile), jnp.float32)
        for f in range(fields):
            for x in range(3):
                j = f * 3 + x
                last = q[s, f, x, rows, width - tile : width]
                first = q[s, f, x, rows, 0:tile]
                high = jnp.where(lane == j, pltpu.roll(last, j + 1, 1), high)
                low = jnp.where(lane == j, pltpu.roll(first, j, 1) if j else first, low)
        flat = pl.ds(pl.multiple_of(k * CH, 8), CH)
        edge_out[0, s, flat, :] = high
        edge_out[1, s, flat, :] = low

    pl.semaphore_wait(barrier, n_gx - 1 + n_gy - 1)
    load_strip.wait()

    owner = owner_ref[gy]
    n_rows, n_half, n_quarter = bound.shape[0], half.shape[0], half.shape[0] // 2
    core = lax.rem(gx, 2)
    far = n_gx // 2
    part = lax.rem(gx // far, 2)

    def flip(bit):
        digit = lax.rem(gx // bit, 2)
        return gx + bit - 2 * bit * digit

    def differs(bit):
        return lax.rem(gx // bit, 2) != lax.rem(owner // bit, 2)

    def b_copy(src, dst, number, bit):
        return pltpu.make_async_remote_copy(
            src_ref=src, dst_ref=dst, send_sem=b_send.at[number], recv_sem=b_recv.at[number],
            device_id={"gx": flip(bit)}, device_id_type=MESH,
        )

    def half_at(c):
        return pl.ds(pl.multiple_of(c * (n_rows - n_half), 8), n_half)

    def quarter_at(c):
        return pl.ds(pl.multiple_of(c * n_quarter, 8), n_quarter)

    step0 = b_copy(strip.at[half_at(1 - core), :], got_half, 0, 1)
    step0.start()
    load.wait()

    def first_sends(k, _):
        send(x_copy, 0, k, 0)
        return 0

    lax.fori_loop(0, chunks, first_sends, 0)
    step0.wait_recv()
    half[...] = jnp.where(differs(1), got_half[...], strip[half_at(core), :])
    step1 = b_copy(half.at[quarter_at(1 - part), :], got_quarter, 1, far)
    step1.start()

    def first_edges(k, _):
        pack(0, k)
        send(y_copy, 0, k, 1)
        return 0

    lax.fori_loop(0, chunks, first_edges, 0)
    step1.wait_recv()
    quarter[0] = jnp.where(differs(far), got_quarter[...], half[quarter_at(part), :])
    pending = [step0, step1]
    bit, i = 2, 0
    while bit < far:
        step = b_copy(quarter.at[i], got_other.at[i], 2 + i, bit)
        step.start()
        step.wait_recv()
        quarter[i + 1] = jnp.where(differs(bit), got_other[i], quarter[i])
        pending.append(step)
        bit, i = bit * 2, i + 1
    whole_half[quarter_at(part), :] = quarter[i]
    step = b_copy(quarter.at[i], whole_half.at[quarter_at(part), :], 2 + i, far)
    step.start()
    step.wait_recv()
    pending.append(step)
    step = b_copy(whole_half, got_rest, 3 + i, 1)
    step.start()
    bound[half_at(core), :] = whole_half[...]
    step.wait_recv()
    pending.append(step)
    bound[half_at(1 - core), :] = got_rest[...]

    wide_lane = lax.broadcasted_iota(jnp.int32, (8, width), 1)
    level = lax.broadcasted_iota(jnp.int32, (8, width), 0)
    is_bottom, is_top = level == 0, level == 7
    is_first, is_last = wide_lane == 0, wide_lane == width - 1

    def block(s, z0, x, weight):
        slope, metric, relax = coef[0, x], coef[1, x], coef[2, x]
        rows = pl.ds(pl.multiple_of(z0 + PAD, 8), 8)
        flat = pl.ds(pl.multiple_of(z0, 8), 8)
        from_south, from_north = edge_in[0, s, flat, :], edge_in[1, s, flat, :]
        centers, axs, ays, azs, commons = [], [], [], [], []
        for f in range(fields):
            c = q[s, f, x, rows, :]
            above = q[s, f, x, pl.ds(pl.multiple_of(z0 + PAD + 8, 8), 8), :]
            below = q[s, f, x, pl.ds(pl.multiple_of(z0 + PAD - 8, 8), 8), :]
            up = pltpu.roll(jnp.where(is_bottom, above, c), 7, 0)
            down = pltpu.roll(jnp.where(is_top, below, c), 1, 0)
            east = q[s, f, x + 1, rows, :] if x < 2 else halo[1, s, f, flat, :]
            west = q[s, f, x - 1, rows, :] if x > 0 else halo[0, s, f, flat, :]
            j = f * 3 + x
            a = pltpu.roll(from_south, tile - j, 1) if j else from_south
            b = pltpu.roll(from_north, tile - 1 - j, 1)
            south = jnp.where(is_first, jnp.concatenate([a] * 3, axis=1), pltpu.roll(c, 1, 1))
            north = jnp.where(is_last, jnp.concatenate([b] * 3, axis=1), pltpu.roll(c, width - 1, 1))
            az = (0.5 * (up - down)) * metric
            ax = 0.5 * (east - west) - slope * az
            ay = 0.5 * (north - south)
            spread = (east + west) + (north + south) - 4.0 * c
            limit = bound[pl.ds(pl.multiple_of(f * levels + z0, 8), 8), :]
            common = relax * (limit - c) + viscosity * spread - (wind_east * ax + wind_north * ay)
            centers.append(c)
            axs.append(ax)
            ays.append(ay)
            azs.append(az)
            commons.append(common)
        tend = [
            commons[0] - axs[4],
            commons[1] - ays[4],
            commons[2] - azs[4] + buoyancy * centers[3],
            commons[3] - buoyancy * centers[2],
            commons[4] - (axs[0] + ays[1] + azs[2]),
        ]
        for f in range(fields):
            q[s + 1, f, x, rows, :] = q[0, f, x, rows, :] + weight * tend[f]

    def out_copy(k):
        rows = pl.ds(pl.multiple_of(k * CH, 8), CH)
        padded = pl.ds(pl.multiple_of(k * CH + PAD, 8), CH)
        return pltpu.make_async_copy(q.at[3, :, :, padded, :], out_ref.at[:, :, rows, :], out_sem.at[k])

    def substep(s, _):
        weight = time_step * jnp.where(s == 0, 1.0 / 3.0, jnp.where(s == 1, 0.5, 1.0)).astype(jnp.float32)

        def chunk(k, _):
            received(y_copy, s, k, 1)
            received(x_copy, s, k, 0)

            def rows8(i, _):
                for x in (0, 2, 1):
                    block(s, k * CH + i * 8, x, weight)
                return 0

            lax.fori_loop(0, CH // 8, rows8, 0)

            @pl.when(s < 2)
            def _():
                send(x_copy, s + 1, k, 0)
                pack(s + 1, k)
                send(y_copy, s + 1, k, 1)

            @pl.when(s == 2)
            def _():
                out_copy(k).start()

            return 0

        lax.fori_loop(0, chunks, chunk, 0)
        return 0

    lax.fori_loop(0, 3, substep, 0)

    feat = 4 * levels
    total[feat:, :] = jnp.zeros((total.shape[0] - feat, width), jnp.float32)
    for i, f in enumerate((0, 1, 3, 4)):
        total[i * levels : (i + 1) * levels, :] = q[3, f, 0, inner, :] + q[3, f, 1, inner, :] + q[3, f, 2, inner, :]
    sub = lax.broadcasted_iota(jnp.int32, (8, width), 0)
    picks, targets = [], []
    for d in range(n_gy):
        pick = jnp.zeros((8, width), jnp.float32)
        target = jnp.full((8, width), -1, jnp.int32)
        for slot in range(cap):
            live = jnp.where(count_ref[d] > slot, slot, -1)
            shifted = wide_lane - 3 * cell_ref[d * cap + slot]
            here = sub == live
            pick = jnp.where(here & (shifted >= 0) & (shifted < 3), 1.0, pick)
            target = jnp.where(here, row_ref[d * cap + slot], target)
        picks.append(pick)
        targets.append(target.astype(jnp.float32))
    pick = jnp.concatenate(picks, axis=0)
    target = jnp.concatenate(targets, axis=0)
    sums = lax.dot_general(
        pick, total[...], (((1,), (1,)), ((), ())), precision=HIGH, preferred_element_type=jnp.float32
    )
    column = lax.broadcasted_iota(jnp.int32, sums.shape, 1)
    records[...] = jnp.where(column == feat, target[:, :1], sums * (1.0 / 9.0))

    def r_copy(off):
        peer = lax.rem(gy + off, n_gy)
        return pltpu.make_async_remote_copy(
            src_ref=records.at[pl.ds(pl.multiple_of(peer * 8, 8), 8), :],
            dst_ref=got_records.at[pl.ds(pl.multiple_of(gy * 8, 8), 8), :],
            send_sem=r_send.at[off - 1],
            recv_sem=r_recv.at[off - 1],
            device_id={"gy": peer},
            device_id_type=MESH,
        )

    for off in range(1, n_gy):
        r_copy(off).start()
    mine = pl.ds(pl.multiple_of(gy * 8, 8), 8)
    got_records[mine, :] = records[mine, :]
    for step in pending:
        step.wait_send()

    def settle(s, _):
        def inner_settle(k, _):
            sent(x_copy, s, k, 0)
            sent(y_copy, s, k, 1)
            return 0

        lax.fori_loop(0, chunks, inner_settle, 0)
        return 0

    lax.fori_loop(0, 3, settle, 0)
    for off in range(1, n_gy):
        r_copy(off).wait()
    got = got_records[...]
    parents = lax.broadcasted_iota(jnp.int32, (got.shape[0], parent_ref.shape[1]), 1).astype(jnp.float32)
    onehot = jnp.where(got[:, feat : feat + 1] == parents, 1.0, 0.0)
    totals = lax.dot_general(
        got, onehot, (((0,), (0,)), ((), ())), precision=HIGH, preferred_element_type=jnp.float32
    )
    tally = jnp.sum(onehot, axis=0, keepdims=True)
    pout_ref[...] = jnp.where(tally > 0, totals[:feat] / jnp.maximum(tally, 1.0), parent_ref[...])

    def settle_out(k, _):
        out_copy(k).wait()
        return 0

    lax.fori_loop(0, chunks, settle_out, 0)


def on_device(
    n_gx, n_gy,
    nest_fields, boundary_strip, strip_owner, terrain_slope, column_metric, relax_rate,
    parent_state, intersection_cell, intersection_row, intersection_count,
):
    fields, levels, cells_x, width = nest_fields.shape
    cap = intersection_cell.shape[3]
    chunks = levels // CH
    n_rows = fields * levels
    n_quarter = -(-n_rows // 32) * 8
    n_half = 2 * n_quarter
    bits = max(n_gx.bit_length() - 3, 1)
    feat = 4 * levels
    feat_pad = -(-(feat + 1) // 128) * 128
    tile = width // 3
    f32 = jnp.float32
    smem = pl.BlockSpec(memory_space=pltpu.SMEM)
    vmem = pl.BlockSpec(memory_space=pltpu.VMEM)
    hbm = pl.BlockSpec(memory_space=pl.ANY)
    dma = pltpu.SemaphoreType.DMA
    out, parent = pl.pallas_call(
        functools.partial(kernel, n_gx, n_gy, cap),
        out_shape=(
            jax.ShapeDtypeStruct((fields, cells_x, levels, width), f32),
            jax.ShapeDtypeStruct((feat, parent_state.shape[1]), f32),
        ),
        in_specs=[smem] * 4 + [hbm] * 2 + [vmem] * 4,
        out_specs=(hbm, vmem),
        scratch_shapes=[
            pltpu.VMEM((4, fields, 3, levels + 2 * PAD, width), f32),
            pltpu.VMEM((2, 3, fields, levels, width), f32),
            pltpu.VMEM((2, 3, levels, tile), f32),
            pltpu.VMEM((2, 3, levels, tile), f32),
            pltpu.VMEM((3, 3, 8, width), f32),
            pltpu.VMEM((n_rows, width), f32),
            pltpu.VMEM((n_half, width), f32),
            pltpu.VMEM((n_half, width), f32),
            pltpu.VMEM((n_quarter, width), f32),
            pltpu.VMEM((bits + 1, n_quarter, width), f32),
            pltpu.VMEM((bits, n_quarter, width), f32),
            pltpu.VMEM((n_half, width), f32),
            pltpu.VMEM((n_half, width), f32),
            pltpu.VMEM((n_rows, width), f32),
            pltpu.VMEM((feat_pad, width), f32),
            pltpu.VMEM((n_gy * 8, feat_pad), f32),
            pltpu.VMEM((n_gy * 8, feat_pad), f32),
            dma,
            dma,
            dma((2, 3, chunks)),
            dma((2, 3, chunks)),
            dma((2, 3, chunks)),
            dma((2, 3, chunks)),
            dma((bits + 4,)),
            dma((bits + 4,)),
            dma((n_gy,)),
            dma((n_gy,)),
            dma((chunks,)),
        ],
        compiler_params=pltpu.CompilerParams(
            collective_id=0, has_side_effects=True, vmem_limit_bytes=40 * 1024 * 1024
        ),
    )(
        strip_owner,
        intersection_cell.reshape(-1),
        intersection_row.reshape(-1),
        intersection_count.reshape(-1),
        nest_fields.transpose(0, 2, 1, 3),
        boundary_strip.reshape(n_rows, width),
        terrain_slope,
        column_metric,
        relax_rate,
        parent_state[0].T,
    )
    return out.transpose(0, 2, 1, 3), parent.T[None]


def solution(mesh):
    placed = (
        P(None, None, "gx", "gy"),
        P("gx", None, None, "gy"),
        P(),
        P("gx", "gy"),
        P("gx", "gy"),
        P("gx", "gy"),
        P("gx", "gy", None),
        P("gx", "gy", None, None),
        P("gx", "gy", None, None),
        P("gx", "gy", None),
    )
    return jax.shard_map(
        functools.partial(on_device, mesh.shape["gx"], mesh.shape["gy"]),
        mesh=mesh,
        in_specs=placed,
        out_specs=(P(None, None, "gx", "gy"), P("gx", "gy", None)),
        check_vma=False,
    )
```

time: 193 us -> 75.9 us (0.39)
  waiting for transfers between devices: 72.3 us -> 0 us
  Pallas kernels: 0 us -> 63.6 us
  starting transfers between devices: 43.4 us -> 0 us
  other arithmetic: 32 us -> 0 us
  local copies, waits for them, and re-layouts: 28.3 us -> 10.3 us
  between operations: 15.2 us -> 0.65 us
    pallas_call x0 -> x1, Pallas kernels: none -> 63.6 us  [on_device(): pl.pallas_call(functools.partial(kernel, n_gx, n_gy, cap), out_shape=(jax...]
    ppermute x12 -> x0, starting transfers between devices: 33.8 us -> none  [the longest x6 22.4 us: padded_2(): before = lax.ppermute(last, axis, up)]
    psum x1 -> x0, waiting for transfers between devices: 33.8 us -> none  [broadcast(): return lax.psum(jnp.where(mine, value, jnp.zeros_like(value)), axis)]
    ppermute x12 -> x0, waiting for transfers between devices: 32.9 us -> none  [the longest x6 24.4 us: padded_2(): before = lax.ppermute(last, axis, up)]
    add x6 -> x0, other arithmetic: 19.4 us -> none  [the longest x3 18.6 us: tendency(): -(wind_east * along_x + wind_north * along_y) + viscosity * spread]
    all_to_all x2 -> x0, starting transfers between devices: 9.62 us -> none  [the longest x1 5.84 us: on_device(): lax.all_to_all(records, 'gy', split_axis=0, concat_axis=0, tiled=True)]
    ppermute x6 -> x0, local copies, waits for them, and re-layouts: 7.37 us -> none  [the longest x3 6.23 us: padded_2(): before = lax.ppermute(last, axis, up)]
    all_to_all x2 -> x0, waiting for transfers between devices: 5.63 us -> none  [the longest x1 5.63 us: on_device(): lax.all_to_all(records, 'gy', split_axis=0, concat_axis=0, tiled=True)]
  transfers between devices with their start and end apart: 15 -> 0, of which waited for: 8 -> 0; matrix products, arithmetic and copies ran while one was open for 15% -> 0% of each run, Pallas kernels for 0% -> 0%
where the time goes in v1:
time: 75.9 us; the launch traced here: 74.5 us
  Pallas kernels  63.6 us (84%)
  local copies, waits for them, and re-layouts  10.3 us (14%)
    pallas_call x1, Pallas kernels, on_device(): pl.pallas_call(functools.partial(kernel, n_gx, n_gy, cap), out_shape=(jax...  63.6 us
    unnamed x18, local copies, waits for them, and re-layouts  8.77 us

profile of v1, /device:TPU:6, one launch (start us, length us, event | category | flops | bytes accessed | tf_op | source)
XLA Modules:
  0.0 74.5 jit_solution(14272459851705678517)
XLA Ops:
  0.6 0.8 %reshape.16.cell_ref = s32[16]{0:T(128)S(1)} reshape(s32[1,1,4,4]{3,2,1,0:T(4,128)} %param.17) | data formatting | bytes 128 | tf_op jit(solution)/shard_map/reshape | solution.py:444
  1.4 0.8 %reshape.17.row_ref = s32[16]{0:T(128)S(1)} reshape(s32[1,1,4,4]{3,2,1,0:T(4,128)} %param.18) | data formatting | bytes 128 | tf_op jit(solution)/shard_map/reshape | solution.py:445
  2.2 0.0 copy-start
  2.2 1.5 %copy-done = f32[5,80,3,384]{3,1,2,0:T(8,128)S(1)} copy-done((f32[5,80,3,384]{3,1,2,0:T(8,128)S(1)}, f32[5,80,3,384]{3,1,2,0:T(8,128)}, u32[]{:S(2)}) %copy-start) | copy-done | bytes 1843224
  3.7 0.0 copy-start.1
  3.7 1.1 %copy-done.1 = f32[1,5,80,384]{3,2,1,0:T(8,128)S(1)} copy-done((f32[1,5,80,384]{3,2,1,0:T(8,128)S(1)}, f32[1,5,80,384]{3,2,1,0:T(8,128)}, u32[]{:S(2)}) %copy-start.1) | copy-done | bytes 614424
  4.7 0.0 copy-start.2
  4.7 0.9 %copy-done.2 = f32[1,128,320]{1,2,0:T(8,128)S(1)} copy-done((f32[1,128,320]{1,2,0:T(8,128)S(1)}, f32[1,128,320]{1,2,0:T(8,128)}, u32[]{:S(2)}) %copy-start.2) | copy-done | bytes 163864
  5.7 0.0 copy-start.3
  5.7 0.7 copy-done.3
  6.3 0.0 copy-start.4
  6.3 0.7 copy-done.4
  7.0 0.0 copy-start.5
  7.0 0.7 copy-done.5
  7.7 0.0 copy-start.6
  7.7 0.7 copy-done.6
  8.4 0.0 copy-start.7
  8.4 0.7 copy-done.7
  9.0 63.6 %shard_map.113 = (f32[5,3,80,384]{3,2,1,0:T(8,128)S(1)}, f32[320,128]{1,0:T(8,128)S(1)}) custom-call(s32[4]{0:T(128)S(1)} %copy-done.6, s32[16]{0:T(128)S(1)} %reshape.16.cell_ref, s32[16]{0:T(128)S(1)} %reshape.17.row_ref, s32[4]{0:T(128)S(1)} %bitcast.15, f32[5,3,80,384]{3,2,1,0:T(8,128)S(1)} %bitcast.10, f32[400,384]{1,0:T(8,128)S(1)} %bitcast.12, ...), custom_call_target="tpu_custom_call" | custom-call | tf_op jit(solution)/shard_map/pallas_call | solution.py:401
  72.6 1.2 %copy.14 = f32[5,80,3,384]{3,1,2,0:T(8,128)} copy(f32[5,80,3,384]{3,1,2,0:T(8,128)S(1)} %bitcast.11) | data formatting | bytes 3686400
  73.9 0.7 copy.15
Async XLA Ops:
  2.2 1.5 %copy-start = (f32[5,80,3,384]{3,1,2,0:T(8,128)S(1)}, f32[5,80,3,384]{3,1,2,0:T(8,128)}, u32[]{:S(2)}) copy-start(f32[5,80,3,384]{3,1,2,0:T(8,128)} %param.10) | copy-start | bytes 5529604
  3.7 1.1 %copy-start.1 = (f32[1,5,80,384]{3,2,1,0:T(8,128)S(1)}, f32[1,5,80,384]{3,2,1,0:T(8,128)}, u32[]{:S(2)}) copy-start(f32[1,5,80,384]{3,2,1,0:T(8,128)} %param.11) | copy-start | bytes 1843204
  4.7 0.9 %copy-start.2 = (f32[1,128,320]{1,2,0:T(8,128)S(1)}, f32[1,128,320]{1,2,0:T(8,128)}, u32[]{:S(2)}) copy-start(f32[1,128,320]{1,2,0:T(8,128)} %param.16) | copy-start | bytes 491524
  5.7 0.7 copy-start.3
  6.3 0.7 copy-start.4
  7.0 0.7 copy-start.5
  7.7 0.7 copy-start.6
  8.4 0.7 copy-start.7

commit v2 on v1

--- a/solution.py
+++ b/solution.py
@@ -14,29 +14,40 @@
 wind_north = -0.4
 PAD = 8
 CH = 16
+PIECES = 2
 HIGH = lax.Precision.HIGHEST
 
 
 def kernel(
-    n_gx, n_gy, cap,
+    n_gx, n_gy, cap, pieces,
     owner_ref, cell_ref, row_ref, count_ref,
-    nest_ref, strip_ref, slope_ref, metric_ref, relax_ref, parent_ref,
+    nest_ref, strip_ref, slope_hbm, metric_hbm, relax_hbm, parent_hbm,
     out_ref, pout_ref,
     q, halo, edge_out, edge_in, coef,
     strip, got_half, half, got_quarter, quarter, got_other, whole_half, got_rest, bound,
-    total, records, got_records,
-    load_sem, strip_sem, x_send, x_recv, y_send, y_recv, b_send, b_recv, r_send, r_recv, out_sem,
+    total, records, got_records, maps, parent_ref,
+    load_sem, strip_sem, x_send, x_recv, y_send, y_recv, b_send, b_recv, r_send, r_recv, out_sem, small_sem,
+    passing, pass_send, pass_recv,
 ):
     fields, levels, width = q.shape[1], q.shape[3] - 2 * PAD, q.shape[4]
     chunks = levels // CH
     gx, gy = lax.axis_index("gx"), lax.axis_index("gy")
     tile = width // 3
     inner = pl.ds(PAD, levels)
+    far = n_gx // 2
 
     load = pltpu.make_async_copy(nest_ref, q.at[0, :, :, inner, :], load_sem)
     load.start()
     load_strip = pltpu.make_async_copy(strip_ref, strip, strip_sem)
     load_strip.start()
+    load_maps = [
+        pltpu.make_async_copy(ref, maps.at[i], small_sem.at[i])
+        for i, ref in enumerate((slope_hbm, metric_hbm, relax_hbm))
+    ]
+    for copy in load_maps:
+        copy.start()
+    load_parent = pltpu.make_async_copy(parent_hbm, parent_ref, small_sem.at[3])
+    load_parent.start()
 
     barrier = pltpu.get_barrier_semaphore()
     for off in range(1, n_gx):
@@ -79,9 +90,10 @@
     def _():
         edge_in[1] = jnp.zeros(edge_in.shape[1:], jnp.float32)
 
-    for x in range(3):
-        for i, ref in enumerate((slope_ref, metric_ref, relax_ref)):
-            coef[i, x] = jnp.broadcast_to(ref[x : x + 1, :], (8, width))
+    for i in range(3):
+        load_maps[i].wait()
+        for x in range(3):
+            coef[i, x] = jnp.broadcast_to(maps[i, x : x + 1, :], (8, width))
 
     has_low = (gx > 0, gy > 0)
     has_high = (gx < n_gx - 1, gy < n_gy - 1)
@@ -111,12 +123,66 @@
             device_id_type=MESH,
         )
 
+    relays = n_gx == 8
+
+    def hop_copy(side, s, k):
+        rows = pl.ds(pl.multiple_of(k * CH, 8), CH)
+        padded = pl.ds(pl.multiple_of(k * CH + PAD, 8), CH)
+        return pltpu.make_async_remote_copy(
+            src_ref=q.at[s, :, 2 if side == 0 else 0, padded, :],
+            dst_ref=passing.at[s, :, rows, :],
+            send_sem=x_send.at[side, s, k],
+            recv_sem=pass_recv.at[s, k],
+            device_id={"gx": gx + far if side == 0 else gx - far},
+            device_id_type=MESH,
+        )
+
+    def pass_copy(side, s, k):
+        rows = pl.ds(pl.multiple_of(k * CH, 8), CH)
+        return pltpu.make_async_remote_copy(
+            src_ref=passing.at[s, :, rows, :],
+            dst_ref=halo.at[side, s, :, rows, :],
+            send_sem=pass_send.at[s, k],
+            recv_sem=x_recv.at[side, s, k],
+            device_id={"gx": far if side == 0 else far - 1},
+            device_id_type=MESH,
+        )
+
+    def forward(s, k):
+        if not relays:
+            return
+
+        @pl.when(gx == n_gx - 1)
+        def _():
+            hop_copy(0, s, k).wait_recv()
+            pass_copy(0, s, k).start()
+
+        @pl.when(gx == 0)
+        def _():
+            hop_copy(1, s, k).wait_recv()
+            pass_copy(1, s, k).start()
+
     def send(copy, s, k, axis):
-        @pl.when(has_high[axis])
+        direct_high, direct_low = has_high[axis], has_low[axis]
+        if axis == 0 and relays:
+            odd = lax.rem(k, 2) == 1
+            hop_high, hop_low = odd & (gx == far - 1), odd & (gx == far)
+            direct_high &= jnp.logical_not(hop_high)
+            direct_low &= jnp.logical_not(hop_low)
+
+            @pl.when(hop_high)
+            def _():
+                hop_copy(0, s, k).start()
+
+            @pl.when(hop_low)
+            def _():
+                hop_copy(1, s, k).start()
+
+        @pl.when(direct_high)
         def _():
             copy(0, s, k).start()
 
-        @pl.when(has_low[axis])
+        @pl.when(direct_low)
         def _():
             copy(1, s, k).start()
 
@@ -159,10 +225,13 @@
     load_strip.wait()
 
     owner = owner_ref[gy]
-    n_rows, n_half, n_quarter = bound.shape[0], half.shape[0], half.shape[0] // 2
+    n_rows = bound.shape[0]
     core = lax.rem(gx, 2)
-    far = n_gx // 2
     part = lax.rem(gx // far, 2)
+    middle = []
+    while 2 << len(middle) < far:
+        middle.append(2 << len(middle))
+    n_phases = 4 + len(middle)
 
     def flip(bit):
         digit = lax.rem(gx // bit, 2)
@@ -171,60 +240,74 @@
     def differs(bit):
         return lax.rem(gx // bit, 2) != lax.rem(owner // bit, 2)
 
-    def b_copy(src, dst, number, bit):
+    def at(start, size):
+        return pl.ds(pl.multiple_of(start, 8), size)
+
+    def b_copy(phase, p):
+        first, count, row = pieces[p]
+        size, base = count * 8, first * 8
+        one, two = at(base, size), at(2 * base, 2 * size)
+        if phase == 0:
+            src, dst, bit = strip.at[at(row + (1 - core) * 2 * size, 2 * size), :], got_half.at[two, :], 1
+        elif phase == 1:
+            src, dst, bit = half.at[at(2 * base + (1 - part) * size, size), :], got_quarter.at[one, :], far
+        elif phase < n_phases - 2:
+            i = phase - 2
+            src, dst, bit = quarter.at[i, one, :], got_other.at[i, one, :], middle[i]
+        elif phase == n_phases - 2:
+            mine = at(2 * base + part * size, size)
+            src, dst, bit = quarter.at[len(middle), one, :], whole_half.at[mine, :], far
+        else:
+            src, dst, bit = whole_half.at[two, :], got_rest.at[two, :], 1
         return pltpu.make_async_remote_copy(
-            src_ref=src, dst_ref=dst, send_sem=b_send.at[number], recv_sem=b_recv.at[number],
+            src_ref=src, dst_ref=dst, send_sem=b_send.at[phase, p], recv_sem=b_recv.at[phase, p],
             device_id={"gx": flip(bit)}, device_id_type=MESH,
         )
 
-    def half_at(c):
-        return pl.ds(pl.multiple_of(c * (n_rows - n_half), 8), n_half)
-
-    def quarter_at(c):
-        return pl.ds(pl.multiple_of(c * n_quarter, 8), n_quarter)
-
-    step0 = b_copy(strip.at[half_at(1 - core), :], got_half, 0, 1)
-    step0.start()
-    load.wait()
+    def b_finish(phase, p):
+        first, count, row = pieces[p]
+        size, base = count * 8, first * 8
+        one, two = at(base, size), at(2 * base, 2 * size)
+        b_copy(phase, p).wait_recv()
+        if phase == 0:
+            half[two, :] = jnp.where(differs(1), got_half[two, :], strip[at(row + core * 2 * size, 2 * size), :])
+        elif phase == 1:
+            quarter[0, one, :] = jnp.where(
+                differs(far), got_quarter[one, :], half[at(2 * base + part * size, size), :]
+            )
+        elif phase < n_phases - 2:
+            i = phase - 2
+            quarter[i + 1, one, :] = jnp.where(differs(middle[i]), got_other[i, one, :], quarter[i, one, :])
+        if phase == n_phases - 3:
+            whole_half[at(2 * base + part * size, size), :] = quarter[len(middle), one, :]
+        if phase < n_phases - 1:
+            b_copy(phase + 1, p).start()
+        if phase == n_phases - 2:
+            bound[at(row + core * 2 * size, 2 * size), :] = whole_half[two, :]
+        elif phase == n_phases - 1:
+            bound[at(row + (1 - core) * 2 * size, 2 * size), :] = got_rest[two, :]
 
     def first_sends(k, _):
         send(x_copy, 0, k, 0)
         return 0
-
-    lax.fori_loop(0, chunks, first_sends, 0)
-    step0.wait_recv()
-    half[...] = jnp.where(differs(1), got_half[...], strip[half_at(core), :])
-    step1 = b_copy(half.at[quarter_at(1 - part), :], got_quarter, 1, far)
-    step1.start()
 
     def first_edges(k, _):
         pack(0, k)
         send(y_copy, 0, k, 1)
         return 0
 
-    lax.fori_loop(0, chunks, first_edges, 0)
-    step1.wait_recv()
-    quarter[0] = jnp.where(differs(far), got_quarter[...], half[quarter_at(part), :])
-    pending = [step0, step1]
-    bit, i = 2, 0
-    while bit < far:
-        step = b_copy(quarter.at[i], got_other.at[i], 2 + i, bit)
-        step.start()
-        step.wait_recv()
-        quarter[i + 1] = jnp.where(differs(bit), got_other[i], quarter[i])
-        pending.append(step)
-        bit, i = bit * 2, i + 1
-    whole_half[quarter_at(part), :] = quarter[i]
-    step = b_copy(quarter.at[i], whole_half.at[quarter_at(part), :], 2 + i, far)
-    step.start()
-    step.wait_recv()
-    pending.append(step)
-    step = b_copy(whole_half, got_rest, 3 + i, 1)
-    step.start()
-    bound[half_at(core), :] = whole_half[...]
-    step.wait_recv()
-    pending.append(step)
-    bound[half_at(1 - core), :] = got_rest[...]
+    for p in range(len(pieces)):
+        b_copy(0, p).start()
+    load.wait()
+    lax.fori_loop(0, chunks, first_sends, 0)
+    for t in range(n_phases + len(pieces) - 1):
+        for phase in reversed(range(n_phases)):
+            if 0 <= t - phase < len(pieces):
+                b_finish(phase, t - phase)
+        if t == 0:
+            lax.fori_loop(0, chunks, first_edges, 0)
+        if t in (2, 4):
+            forward(0, t - 1)
 
     wide_lane = lax.broadcasted_iota(jnp.int32, (8, width), 1)
     level = lax.broadcasted_iota(jnp.int32, (8, width), 0)
@@ -295,6 +378,11 @@
                 send(x_copy, s + 1, k, 0)
                 pack(s + 1, k)
                 send(y_copy, s + 1, k, 1)
+                if relays:
+
+                    @pl.when((k > 1) & (lax.rem(k, 2) == 0))
+                    def _():
+                        forward(s + 1, k - 1)
 
             @pl.when(s == 2)
             def _():
@@ -317,11 +405,11 @@
         pick = jnp.zeros((8, width), jnp.float32)
         target = jnp.full((8, width), -1, jnp.int32)
         for slot in range(cap):
-            live = jnp.where(count_ref[d] > slot, slot, -1)
-            shifted = wide_lane - 3 * cell_ref[d * cap + slot]
+            live = jnp.where(count_ref[0, 0, d] > slot, slot, -1)
+            shifted = wide_lane - 3 * cell_ref[0, 0, d, slot]
             here = sub == live
             pick = jnp.where(here & (shifted >= 0) & (shifted < 3), 1.0, pick)
-            target = jnp.where(here, row_ref[d * cap + slot], target)
+            target = jnp.where(here, row_ref[0, 0, d, slot], target)
         picks.append(pick)
         targets.append(target.astype(jnp.float32))
     pick = jnp.concatenate(picks, axis=0)
@@ -347,13 +435,19 @@
         r_copy(off).start()
     mine = pl.ds(pl.multiple_of(gy * 8, 8), 8)
     got_records[mine, :] = records[mine, :]
-    for step in pending:
-        step.wait_send()
+    for p in range(len(pieces)):
+        for phase in range(n_phases):
+            b_copy(phase, p).wait_send()
 
     def settle(s, _):
         def inner_settle(k, _):
             sent(x_copy, s, k, 0)
             sent(y_copy, s, k, 1)
+            if relays:
+
+                @pl.when((lax.rem(k, 2) == 1) & ((gx == 0) | (gx == n_gx - 1)))
+                def _():
+                    pass_copy(0, s, k).wait_send()
             return 0
 
         lax.fori_loop(0, chunks, inner_settle, 0)
@@ -368,6 +462,7 @@
     totals = lax.dot_general(
         got, onehot, (((0,), (0,)), ((), ())), precision=HIGH, preferred_element_type=jnp.float32
     )
+    load_parent.wait()
     tally = jnp.sum(onehot, axis=0, keepdims=True)
     pout_ref[...] = jnp.where(tally > 0, totals[:feat] / jnp.maximum(tally, 1.0), parent_ref[...])
 
@@ -387,7 +482,13 @@
     cap = intersection_cell.shape[3]
     chunks = levels // CH
     n_rows = fields * levels
-    n_quarter = -(-n_rows // 32) * 8
+    quarters = -(-n_rows // 32)
+    pieces = []
+    for p in range(PIECES):
+        first = quarters * p // PIECES
+        count = quarters * (p + 1) // PIECES - first
+        pieces.append((first, count, min(first * 32, n_rows - count * 32)))
+    n_quarter = quarters * 8
     n_half = 2 * n_quarter
     bits = max(n_gx.bit_length() - 3, 1)
     feat = 4 * levels
@@ -399,12 +500,12 @@
     hbm = pl.BlockSpec(memory_space=pl.ANY)
     dma = pltpu.SemaphoreType.DMA
     out, parent = pl.pallas_call(
-        functools.partial(kernel, n_gx, n_gy, cap),
+        functools.partial(kernel, n_gx, n_gy, cap, tuple(pieces)),
         out_shape=(
             jax.ShapeDtypeStruct((fields, cells_x, levels, width), f32),
             jax.ShapeDtypeStruct((feat, parent_state.shape[1]), f32),
         ),
-        in_specs=[smem] * 4 + [hbm] * 2 + [vmem] * 4,
+        in_specs=[smem] * 4 + [hbm] * 6,
         out_specs=(hbm, vmem),
         scratch_shapes=[
             pltpu.VMEM((4, fields, 3, levels + 2 * PAD, width), f32),
@@ -424,26 +525,32 @@
             pltpu.VMEM((feat_pad, width), f32),
             pltpu.VMEM((n_gy * 8, feat_pad), f32),
             pltpu.VMEM((n_gy * 8, feat_pad), f32),
+            pltpu.VMEM((3, 3, width), f32),
+            pltpu.VMEM((feat, parent_state.shape[1]), f32),
             dma,
             dma,
             dma((2, 3, chunks)),
             dma((2, 3, chunks)),
             dma((2, 3, chunks)),
             dma((2, 3, chunks)),
-            dma((bits + 4,)),
-            dma((bits + 4,)),
+            dma((bits + 4, PIECES)),
+            dma((bits + 4, PIECES)),
             dma((n_gy,)),
             dma((n_gy,)),
             dma((chunks,)),
+            dma((4,)),
+            pltpu.VMEM((3, fields, levels, width), f32),
+            dma((3, chunks)),
+            dma((3, chunks)),
         ],
         compiler_params=pltpu.CompilerParams(
-            collective_id=0, has_side_effects=True, vmem_limit_bytes=40 * 1024 * 1024
+            collective_id=0, has_side_effects=True, vmem_limit_bytes=62 * 1024 * 1024
         ),
     )(
         strip_owner,
-        intersection_cell.reshape(-1),
-        intersection_row.reshape(-1),
-        intersection_count.reshape(-1),
+        intersection_cell,
+        intersection_row,
+        intersection_count,
         nest_fields.transpose(0, 2, 1, 3),
         boundary_strip.reshape(n_rows, width),
         terrain_slope,

time: 75.9 us -> 61.1 us (0.81)
  Pallas kernels: 63.6 us -> 55.8 us
  local copies, waits for them, and re-layouts: 10.3 us -> 3.56 us
    pallas_call x1, Pallas kernels: 63.6 us -> 55.8 us  [on_device(): pl.pallas_call(functools.partial(kernel, n_gx, n_gy, cap, tuple(pieces)),...]
    unnamed x18 -> x4, local copies, waits for them, and re-layouts: 8.77 us -> 3.56 us
    reshape x2 -> x0, local copies, waits for them, and re-layouts: 1.53 us -> none  [the longest x1 0.76 us: on_device(): intersection_row.reshape(-1)]
where the time goes in v2:
time: 61.1 us; the launch traced here: 60 us
  Pallas kernels  55.8 us (91%)
  local copies, waits for them, and re-layouts  3.56 us (6%)
  between operations  0.65 us (1%)
    pallas_call x1, Pallas kernels, on_device(): pl.pallas_call(functools.partial(kernel, n_gx, n_gy, cap, tuple(pieces)),...  55.8 us
    unnamed x4, local copies, waits for them, and re-layouts  3.56 us

profile of v2, /device:TPU:6, one launch (start us, length us, event | category | flops | bytes accessed | tf_op | source)
XLA Modules:
  0.0 60.0 jit_solution(11856986223337574281)
XLA Ops:
  0.6 55.8 %shard_map.113 = (f32[5,3,80,384]{3,2,1,0:T(8,128)}, f32[320,128]{1,0:T(8,128)}) custom-call(s32[4]{0:T(128)} %owner_ref.1, s32[1,1,4,4]{3,2,1,0:T(4,128)} %cell_ref.1, s32[1,1,4,4]{3,2,1,0:T(4,128)} %row_ref.1, s32[1,1,4]{2,1,0:T(1,128)} %count_ref.1, f32[5,3,80,384]{3,2,1,0:T(8,128)} %bitcast.10, f32[400,384]{1,0:T(8,128)} %bitcast.11, ...), custom_call_target="tpu_custom_call" | custom-call | tf_op jit(solution)/shard_map/pallas_call | solution.py:502
  56.5 0.0 copy-start
  56.5 2.9 %copy.14 = f32[5,80,3,384]{3,1,2,0:T(8,128)} copy(f32[5,80,3,384]{3,1,2,0:T(8,128)} %bitcast.9) | data formatting | bytes 3686400
  59.4 0.0 copy-done
  59.4 0.7 %copy.15 = f32[1,128,320]{1,2,0:T(8,128)} copy(f32[1,128,320]{1,2,0:T(8,128)S(1)} %bitcast.13) | data formatting | bytes 327680
Async XLA Ops:
  56.5 2.9 %copy-start = (f32[320,128]{1,0:T(8,128)S(1)}, f32[320,128]{1,0:T(8,128)}, u32[]{:S(2)}) copy-start(f32[320,128]{1,0:T(8,128)} %get-tuple-element.5) | copy-start | bytes 491524

commit v3 on v2

--- a/solution.py
+++ b/solution.py
@@ -299,11 +299,14 @@
     for p in range(len(pieces)):
         b_copy(0, p).start()
     load.wait()
-    lax.fori_loop(0, chunks, first_sends, 0)
+    send(x_copy, 0, 0, 0)
+    send(x_copy, 0, 1, 0)
     for t in range(n_phases + len(pieces) - 1):
         for phase in reversed(range(n_phases)):
             if 0 <= t - phase < len(pieces):
                 b_finish(phase, t - phase)
+        if 0 < t < chunks - 1:
+            send(x_copy, 0, t + 1, 0)
         if t == 0:
             lax.fori_loop(0, chunks, first_edges, 0)
         if t in (2, 4):
@@ -363,15 +366,19 @@
         weight = time_step * jnp.where(s == 0, 1.0 / 3.0, jnp.where(s == 1, 0.5, 1.0)).astype(jnp.float32)
 
         def chunk(k, _):
-            received(y_copy, s, k, 1)
-            received(x_copy, s, k, 0)
-
-            def rows8(i, _):
-                for x in (0, 2, 1):
+            def middle_rows(i, _):
+                block(s, k * CH + i * 8, 1, weight)
+                return 0
+
+            def outer_rows(i, _):
+                for x in (0, 2):
                     block(s, k * CH + i * 8, x, weight)
                 return 0
 
-            lax.fori_loop(0, CH // 8, rows8, 0)
+            received(y_copy, s, k, 1)
+            lax.fori_loop(0, CH // 8, middle_rows, 0)
+            received(x_copy, s, k, 0)
+            lax.fori_loop(0, CH // 8, outer_rows, 0)
 
             @pl.when(s < 2)
             def _():

time: 61.1 us -> 59 us (0.966)
  Pallas kernels: 55.8 us -> 54.1 us
    pallas_call x1, Pallas kernels: 55.8 us -> 54.1 us  [on_device(): pl.pallas_call(functools.partial(kernel, n_gx, n_gy, cap, tuple(pieces)),...]
where the time goes in v3:
time: 59 us; the launch traced here: 58.3 us
  Pallas kernels  54.1 us (92%)
  local copies, waits for them, and re-layouts  3.56 us (6%)
  between operations  0.65 us (1%)
    pallas_call x1, Pallas kernels, on_device(): pl.pallas_call(functools.partial(kernel, n_gx, n_gy, cap, tuple(pieces)),...  54.1 us
    unnamed x4, local copies, waits for them, and re-layouts  3.56 us

profile of v3, /device:TPU:6, one launch (start us, length us, event | category | flops | bytes accessed | tf_op | source)
XLA Modules:
  0.0 58.3 jit_solution(7624091498306695179)
XLA Ops:
  0.6 54.1 %shard_map.113 = (f32[5,3,80,384]{3,2,1,0:T(8,128)}, f32[320,128]{1,0:T(8,128)}) custom-call(s32[4]{0:T(128)} %owner_ref.1, s32[1,1,4,4]{3,2,1,0:T(4,128)} %cell_ref.1, s32[1,1,4,4]{3,2,1,0:T(4,128)} %row_ref.1, s32[1,1,4]{2,1,0:T(1,128)} %count_ref.1, f32[5,3,80,384]{3,2,1,0:T(8,128)} %bitcast.10, f32[400,384]{1,0:T(8,128)} %bitcast.11, ...), custom_call_target="tpu_custom_call" | custom-call | tf_op jit(solution)/shard_map/pallas_call | solution.py:509
  54.8 0.0 copy-start
  54.8 2.9 %copy.14 = f32[5,80,3,384]{3,1,2,0:T(8,128)} copy(f32[5,80,3,384]{3,1,2,0:T(8,128)} %bitcast.9) | data formatting | bytes 3686400
  57.7 0.0 copy-done
  57.7 0.7 %copy.15 = f32[1,128,320]{1,2,0:T(8,128)} copy(f32[1,128,320]{1,2,0:T(8,128)S(1)} %bitcast.13) | data formatting | bytes 327680
Async XLA Ops:
  54.8 2.9 %copy-start = (f32[320,128]{1,0:T(8,128)S(1)}, f32[320,128]{1,0:T(8,128)}, u32[]{:S(2)}) copy-start(f32[320,128]{1,0:T(8,128)} %get-tuple-element.5) | copy-start | bytes 491524
